TPU v7x, 32 devices: a whole 2x2x4 slice. The times are simulated.
32 devices in a mesh: groups: 2 (over y), wide: 4 (over z), narrow: 4 (over x, core).
Axes of the slice: x: 2, y: 2, z: 4, core: 2. Of those that a mesh axis runs over, the one named last changes fastest.
Arguments:
- populations: float32 [19, 96, 192, 128], P(None, ('groups', 'wide'), 'narrow'), parts along dimension 1, may hold values from 0.008 to 0.57, as said below
- flags: int32 [96, 192, 128], P(('groups', 'wide'), 'narrow'), parts along dimension 0, may hold values from 0 to 3, as said below
- potential: float32 [24, 48, 32], P(('groups', 'wide'), 'narrow'), parts along dimension 0, may hold values from -6 to 6
- conductivity: float32 [24, 48, 32], P(('groups', 'wide'), 'narrow'), parts along dimension 0, may hold values from 0.5 to 2
- coil_phase: int32 [24, 48, 32], P(('groups', 'wide'), 'narrow'), parts along dimension 0, may hold values from 0 to 2
- phase_table: float32 [3, 4], replicated, may hold values from -4 to 4
- magnetic: float32 [3, 24, 48, 32], P(None, ('groups', 'wide'), 'narrow'), parts along dimension 1, may hold values from -6 to 6
Outputs:
- populations_out: float32 [19, 96, 192, 128], P(None, ('groups', 'wide'), 'narrow'), parts along dimension 1
- potential_out: float32 [24, 48, 32], P(('groups', 'wide'), 'narrow'), parts along dimension 0
- lorentz: float32 [3, 24, 48, 32], P(None, ('groups', 'wide'), 'narrow'), parts along dimension 1
There are 2 independent parts, one for each index of `groups`. A program takes and returns all parts, laid end to end along the dimension named above; an argument that names none is the same for every part. Nothing has to cross between parts.
Inputs may be any that keep to these rules, and one draw needn't show every extreme that they name: flags: 0 fluid, 1 wall, 2 inlet, 3 outlet. `populations`: each population is its lattice weight times a positive factor.
All inputs are finite; a program needn't handle non-finite values.
Results may differ from a plain program's by a relative error of at most 0.00002.
Values sent between devices are 32-bit elements; how exact they have to be, the bound alone decides.
A program may use at most 64 MiB of HBM per device.

v0:
```python
import functools

import jax
import jax.numpy as jnp
from jax import lax
from jax.experimental import pallas as pl
from jax.experimental.pallas import tpu as pltpu
from jax.sharding import PartitionSpec as P

SWEEPS = 2
REACH = 3
SIDE = 8

lattice_dirs = [
    (0, 0, 0),
    (1, 0, 0),
    (-1, 0, 0),
    (0, 1, 0),
    (0, -1, 0),
    (0, 0, 1),
    (0, 0, -1),
    (1, 1, 0),
    (-1, -1, 0),
    (1, -1, 0),
    (-1, 1, 0),
    (1, 0, 1),
    (-1, 0, -1),
    (1, 0, -1),
    (-1, 0, 1),
    (0, 1, 1),
    (0, -1, -1),
    (0, 1, -1),
    (0, -1, 1),
]
opposite_dir = [0, 2, 1, 4, 3, 6, 5, 8, 7, 10, 9, 12, 11, 14, 13, 16, 15, 18, 17]
lattice_weights = [1.0 / 3.0] + [1.0 / 18.0] * 6 + [1.0 / 36.0] * 12
relax_time = 0.8
force_scale = 0.02
inlet_speed = 0.05

flat = [i for i in range(19) if lattice_dirs[i][2] == 0]
rising = [i for i in range(19) if lattice_dirs[i][2] == 1]
sinking = [i for i in range(19) if lattice_dirs[i][2] == -1]
slot_of = {number: place for place, number in enumerate(flat + rising + sinking)}
leaving_y = {
    1: [i for i in range(19) if lattice_dirs[i][1] == 1],
    -1: [i for i in range(19) if lattice_dirs[i][1] == -1],
}
corner_of = {
    (dz, dy): [i for i in range(19) if lattice_dirs[i] == (0, dy, dz)][0]
    for dz in (-1, 1)
    for dy in (-1, 1)
}
ways = [(1, 0), (-1, 0), (0, 1), (0, -1), (1, 1), (1, -1), (-1, 1), (-1, -1)]


def plus(a, b):
    if a is None:
        return b
    if b is None:
        return a
    return a + b


def signed_sum(steps, parts):
    total = None
    for step, part in zip(steps, parts):
        if step != 0:
            total = plus(total, part if step > 0 else -part)
    return total


def exchange_kernel(
    pop_hbm, flags_hbm, pot_hbm, cond_hbm, coil_hbm, mag_hbm, table_hbm,
    post, words, pot_out, lor_out,
    popv, pot, cond, coil, mag, table, coarse, rim, cells, bits_x, bits_xy,
    ysend, yrecv, lor_rows, force,
    in_sems, coarse_send, coarse_recv, flag_send, flag_recv, post_send, post_recv,
):
    size_z, size_y, size_x = flags_hbm.shape
    rough_z, rough_y, rough_x = pot.shape
    tiles = size_y // 8
    up_z, up_y, up_x = size_z // rough_z, size_y // rough_y, size_x // rough_x
    at_z, at_y = lax.axis_index("wide"), lax.axis_index("narrow")
    num_z, num_y = lax.axis_size("wide"), lax.axis_size("narrow")

    def has(dz, dy):
        inside = None
        for step, place, count in ((dz, at_z, num_z), (dy, at_y, num_y)):
            if step != 0:
                this = place < count - 1 if step > 0 else place > 0
                inside = this if inside is None else jnp.logical_and(inside, this)
        return inside

    def target(dz, dy):
        return {"wide": at_z + dz, "narrow": at_y + dy}

    smalls = []
    for number, (src, dst) in enumerate(
        [(pot_hbm, pot), (cond_hbm, cond), (coil_hbm, coil), (table_hbm, table),
         (flags_hbm, cells.at[pl.ds(1, size_z), pl.ds(SIDE, size_y)]), (mag_hbm, mag)]
    ):
        copy = pltpu.make_async_copy(src, dst, in_sems.at[3 + number])
        copy.start()
        smalls.append(copy)
    loads = []
    spans = [(0, 1), (size_z - 1, 1), (1, size_z - 2)]
    for number, (first, count) in enumerate(spans):
        copy = pltpu.make_async_copy(
            pop_hbm.at[:, pl.ds(first, count)], popv.at[:, pl.ds(first, count)], in_sems.at[number]
        )
        copy.start()
        loads.append(copy)

    rim[...] = jnp.zeros(rim.shape, jnp.float32)
    rows_ext = cells.shape[1]
    for layer in (0, size_z + 1):
        cells[layer] = jnp.ones((rows_ext, size_x), jnp.int32)
    for first in (0, SIDE + size_y):
        cells[1 : size_z + 1, first : first + SIDE] = jnp.ones((size_z, SIDE, size_x), jnp.int32)

    barrier = pltpu.get_barrier_semaphore()
    for way in ways:
        @pl.when(has(*way))
        def _(way=way):
            pl.semaphore_signal(
                barrier, inc=1, device_id=target(*way), device_id_type=pl.DeviceIdType.MESH
            )

    coarse[...] = jnp.zeros(coarse.shape, jnp.float32)
    lor_rows[...] = jnp.zeros(lor_rows.shape, jnp.float32)

    for copy in smalls[:4]:
        copy.wait()

    def looked_up(column):
        phase = coil[...]
        summed = jnp.zeros(phase.shape, jnp.float32)
        for number in range(3):
            summed = summed + jnp.where(phase == number, table[number : number + 1, column : column + 1], jnp.float32(0.0))
        return summed

    lanes3 = lax.broadcasted_iota(jnp.int32, coarse.shape, 2)
    coarse[:, 0:rough_y, 0:rough_x] = cond[...] * looked_up(0)
    moved = pltpu.roll(coarse[...], rough_x, 2)
    coarse[:, 0:rough_y, 0:rough_x] = pot[...]
    coarse[...] = jnp.where(lanes3 < rough_x, coarse[...], moved)

    def rough_copy(number):
        dz, dy = ways[number]
        layers = {0: (0, rough_z), 1: (rough_z - 2, 2), -1: (0, 2)}[dz] if dy != 0 else (0, rough_z)
        rows = {0: (0, 16), 1: (8, 8), -1: (0, 8)}[dy]
        return pltpu.make_async_remote_copy(
            src_ref=coarse.at[pl.ds(*layers), pl.ds(*rows)],
            dst_ref=rim.at[number, pl.ds(*layers), pl.ds(0, rows[1])],
            send_sem=coarse_send.at[number],
            recv_sem=coarse_recv.at[number],
            device_id=target(dz, dy),
            device_id_type=pl.DeviceIdType.MESH,
        )

    def flag_copy(number):
        dz, dy = ways[number]
        src_z = {0: (0, size_z), 1: (size_z - 1, 1), -1: (0, 1)}[dz]
        dst_z = {0: 1, 1: 0, -1: size_z + 1}[dz]
        src_y = {0: (0, size_y), 1: (size_y - SIDE, SIDE), -1: (0, SIDE)}[dy]
        dst_y = {0: SIDE, 1: 0, -1: SIDE + size_y}[dy]
        return pltpu.make_async_remote_copy(
            src_ref=cells.at[pl.ds(src_z[0] + 1, src_z[1]), pl.ds(src_y[0] + SIDE, src_y[1])],
            dst_ref=cells.at[pl.ds(dst_z, src_z[1]), pl.ds(dst_y, src_y[1])],
            send_sem=flag_send.at[number],
            recv_sem=flag_recv.at[number],
            device_id=target(dz, dy),
            device_id_type=pl.DeviceIdType.MESH,
        )

    def post_copy(number):
        dz, dy = ways[number]
        if dz == 0:
            side = 0 if dy > 0 else 1
            src, dst = ysend.at[side], yrecv.at[side]
        else:
            src_layer = size_z if dz > 0 else 1
            dst_layer = 0 if dz > 0 else size_z + 1
            if dy == 0:
                group = rising if dz > 0 else sinking
                held = pl.ds(slot_of[group[0]], len(group))
                src = post.at[held, src_layer, pl.ds(SIDE, size_y)]
                dst = post.at[held, dst_layer, pl.ds(SIDE, size_y)]
            else:
                slot = slot_of[corner_of[(dz, dy)]]
                src_row, dst_row = (size_y, 0) if dy > 0 else (SIDE, SIDE + size_y)
                src = post.at[slot, src_layer, pl.ds(src_row, SIDE)]
                dst = post.at[slot, dst_layer, pl.ds(dst_row, SIDE)]
        return pltpu.make_async_remote_copy(
            src_ref=src,
            dst_ref=dst,
            send_sem=post_send.at[number],
            recv_sem=post_recv.at[number],
            device_id=target(dz, dy),
            device_id_type=pl.DeviceIdType.MESH,
        )

    def start(make, number):
        @pl.when(has(*ways[number]))
        def _():
            make(number).start()

    def wait_sent(make, number):
        @pl.when(has(*ways[number]))
        def _():
            make(number).wait_send()

    def wait_received(make, number):
        dz, dy = ways[number]

        @pl.when(has(-dz, -dy))
        def _():
            make(number).wait_recv()

    beside_z = (at_z > 0).astype(jnp.int32) + (at_z < num_z - 1).astype(jnp.int32)
    beside_y = (at_y > 0).astype(jnp.int32) + (at_y < num_y - 1).astype(jnp.int32)
    pl.semaphore_wait(barrier, (beside_z + 1) * (beside_y + 1) - 1)

    for number in range(8):
        start(rough_copy, number)
    smalls[4].wait()
    for number in range(8):
        start(flag_copy, number)
    smalls[5].wait()

    for number in range(8):
        wait_received(rough_copy, number)

    tall = 3 * 8
    row = lax.broadcasted_iota(jnp.int32, (tall, 128), 0)
    lane = lax.broadcasted_iota(jnp.int32, (tall, 128), 1)
    sub = lax.broadcasted_iota(jnp.int32, (8, 128), 0)
    row_all = at_y * rough_y + row - 8
    shown = (lane < rough_x) & (row_all >= 0) & (row_all < num_y * rough_y)
    blocks = {}
    number_of = {way: number for number, way in enumerate(ways)}
    gap = 16 - rough_y
    for dz in (-1, 0, 1):
        for layer in range(rough_z):
            if dz == 0:
                low, high = coarse[layer, 0:8], coarse[layer, 8:16]
            else:
                middle = number_of[(-dz, 0)]
                low, high = rim[middle, layer, 0:8], rim[middle, layer, 8:16]
            before = rim[number_of[(-dz, 1)], layer, 0:8]
            after = rim[number_of[(-dz, -1)], layer, 0:8]
            before = pltpu.roll(before, gap, 0)
            after = jnp.where(sub < rough_y - 8, high, pltpu.roll(after, rough_y - 8, 0))
            blocks[dz * rough_z + layer] = jnp.concatenate([before, low, after], axis=0)
    places = list(range(-REACH, rough_z + REACH))
    field = {p: jnp.where(shown, blocks[p], 0.0) for p in places}
    layer_all = {p: at_z * rough_z + p for p in places}

    def around(v):
        return (
            pltpu.roll(v, 1, 0), pltpu.roll(v, tall - 1, 0), pltpu.roll(v, 1, 1), pltpu.roll(v, 127, 1)
        )

    for sweep in range(SWEEPS):
        fresh = {}
        for p in places[sweep + 1 : len(places) - sweep - 1]:
            back_y, next_y, back_x, next_x = around(field[p])
            source = pltpu.roll(blocks[p], 128 - rough_x, 1)
            total = field[p + 1] + field[p - 1] + next_y + back_y + next_x + back_x + source
            inside = shown & (layer_all[p] >= 0) & (layer_all[p] < num_z * rough_z)
            fresh[p] = jnp.where(inside, total * jnp.float32(1.0 / 6.0), 0.0)
        field = fresh
    held_phase = [looked_up(1 + a) for a in range(3)]
    for layer in range(rough_z):
        back_y, next_y, back_x, next_x = around(field[layer])
        grads = (
            (next_x - back_x) * 0.5, (next_y - back_y) * 0.5, (field[layer + 1] - field[layer - 1]) * 0.5
        )
        pot_out[layer] = field[layer][8 : 8 + rough_y, 0:rough_x]
        cur = [
            cond[layer] * (held_phase[a][layer] - grads[a][8 : 8 + rough_y, 0:rough_x])
            for a in range(3)
        ]
        for a in range(3):
            b, c = (a + 1) % 3, (a + 2) % 3
            value = cur[b] * mag[c, layer] - cur[c] * mag[b, layer]
            lor_out[a, layer] = value
            lor_rows[a * rough_z + layer, 0:rough_y, 0:rough_x] = value

    spread_from = lax.broadcasted_iota(jnp.int32, (128, size_x), 0)
    spread_to = lax.broadcasted_iota(jnp.int32, (128, size_x), 1)
    first_lane = spread_from * up_x
    spread = ((spread_to >= first_lane) & (spread_to < first_lane + up_x)).astype(jnp.float32)
    wide_rows = jnp.dot(
        lor_rows[...].reshape(3 * rough_z * 16, 128),
        spread,
        precision=lax.Precision.HIGHEST,
        preferred_element_type=jnp.float32,
    ) * force_scale
    wide_sub = lax.broadcasted_iota(jnp.int32, (8, size_x), 0)
    for place in range(3 * rough_z):
        for tile in range(tiles):
            value = None
            for part in range(8 // up_y):
                at = place * 16 + tile * (8 // up_y) + part
                line = jnp.broadcast_to(wide_rows[at : at + 1], (8, size_x))
                value = line if value is None else jnp.where(wide_sub < part * up_y, value, line)
            force[place // rough_z, place % rough_z, tile * 8 : tile * 8 + 8] = value

    share = 1.0 - 0.5 / relax_time
    keep = 1.0 - 1.0 / relax_time

    def block(at, first, edge):
        rows = pl.ds(first, 8)
        out_rows = pl.ds(first + SIDE, 8)
        f = [popv[i, at, rows] for i in range(19)]
        kind = cells[at + 1, out_rows]
        forces = [force[a, lax.div(at, up_z), rows] for a in range(3)]
        fluid = kind == 0
        wall = kind == 1
        inlet = kind == 2
        density = f[0]
        mom = [None, None, None]
        for i in range(1, 19, 2):
            both = f[i] + f[i + 1]
            apart = f[i] - f[i + 1]
            density = density + both
            for a in range(3):
                step = lattice_dirs[i][a]
                if step != 0:
                    part = apart if step > 0 else -apart
                    mom[a] = part if mom[a] is None else (
                        mom[a] + apart if step > 0 else mom[a] - apart
                    )
        inverse = 1.0 / density
        still = (0.0, 0.0, -inlet_speed)
        vel = [
            jnp.where(inlet, jnp.float32(still[a]), (mom[a] + 0.5 * forces[a]) * inverse)
            for a in range(3)
        ]
        scale = jnp.where(fluid, density * (1.0 / relax_time), jnp.where(wall, 0.0, 1.0))
        kept = jnp.where(fluid, jnp.float32(keep), jnp.where(wall, 1.0, 0.0))
        push = [jnp.where(fluid, (3.0 * share) * forces[a], 0.0) for a in range(3)]
        square = vel[0] * vel[0] + vel[1] * vel[1] + vel[2] * vel[2]
        work = vel[0] * push[0] + vel[1] * push[1] + vel[2] * push[2]
        base = scale - (1.5 * scale) * square - work
        scale3 = 3.0 * scale
        result = [None] * 19
        result[0] = kept * f[0] + lattice_weights[0] * base
        based = {w: w * base for w in set(lattice_weights[1:])}
        for i in range(1, 19, 2):
            w = lattice_weights[i]
            along_u = signed_sum(lattice_dirs[i], vel)
            along_f = signed_sum(lattice_dirs[i], push)
            odd = scale3 * along_u + along_f
            even = based[w] + (1.5 * w) * along_u * (odd + along_f)
            odd = w * odd
            one, two = kept * f[i], kept * f[i + 1]
            one, two = jnp.where(wall, two, one), jnp.where(wall, one, two)
            result[i] = one + (even + odd)
            result[i + 1] = two + (even - odd)
        for i in range(19):
            post[slot_of[i], at + 1, out_rows] = result[i]
        if edge != 0:
            side, pick = (0, 7) if edge > 0 else (1, 0)
            for k, i in enumerate(leaving_y[edge]):
                ysend[side, k, pl.ds(at, 1)] = result[i][pick : pick + 1]

    last = size_y - 8
    loads[0].wait()
    loads[1].wait()

    def ends(turn, carry):
        at = turn * (size_z - 1)
        block(at, 0, -1)
        for tile in range(1, tiles - 1):
            block(at, tile * 8, 0)
        block(at, last, 1)
        return carry

    lax.fori_loop(0, 2, ends, 0)
    for number, way in enumerate(ways):
        if way[0] != 0:
            start(post_copy, number)
    loads[2].wait()

    def sides(at, carry):
        block(at, 0, -1)
        block(at, last, 1)
        return carry

    lax.fori_loop(1, size_z - 1, sides, 0)
    for number, way in enumerate(ways):
        if way[0] == 0:
            start(post_copy, number)

    def middles(at, carry):
        for tile in range(1, tiles - 1):
            block(at, tile * 8, 0)
        return carry

    lax.fori_loop(1, size_z - 1, middles, 0)

    for number in range(8):
        wait_received(flag_copy, number)
    end_lane = lax.broadcasted_iota(jnp.int32, (rows_ext, size_x), 1)

    def opens(layer, carry):
        state = jnp.where(cells[layer] != 1, 1, 0)
        back = jnp.where(end_lane > 0, pltpu.roll(state, 1, 1), 0)
        ahead = jnp.where(end_lane < size_x - 1, pltpu.roll(state, size_x - 1, 1), 0)
        bits_x[...] = state + 2 * back + 4 * ahead
        near = bits_x[SIDE - 1 : SIDE - 1 + size_y], bits_x[SIDE + 1 : SIDE + 1 + size_y]
        bits_xy[layer] = bits_x[SIDE : SIDE + size_y] + 8 * near[0] + 64 * near[1]
        return carry

    lax.fori_loop(0, size_z + 2, opens, 0)

    def join(at, carry):
        here = bits_xy[at + 1]
        word = here + 512 * bits_xy[at] + 262144 * bits_xy[at + 2]
        words[at] = jnp.where((here & 1) != 0, word, 0)
        return carry

    lax.fori_loop(0, size_z, join, 0)

    for number in range(8):
        wait_received(post_copy, number)
    for way, row_at in ((1, SIDE - 1), (-1, SIDE + size_y)):
        side = 0 if way > 0 else 1
        for k, i in enumerate(leaving_y[way]):
            for layer in range(size_z):
                post[slot_of[i], layer + 1, row_at : row_at + 1] = yrecv[side, k, layer : layer + 1]

    for number in range(8):
        wait_sent(rough_copy, number)
        wait_sent(flag_copy, number)
        wait_sent(post_copy, number)


def bit_of(step_x, step_y, step_z):
    place = {0: 0, 1: 1, -1: 2}
    return 1 << (place[step_x] + 3 * place[step_y] + 9 * place[step_z])


def stream_kernel(post, words, pot_in, lor_in, out, pot_out, lor_out, held, sems, small_sems):
    size_z, size_y, size_x = words.shape
    own = pl.ds(SIDE, size_y)
    smalls = [
        pltpu.make_async_copy(pot_in, pot_out, small_sems.at[0]),
        pltpu.make_async_copy(lor_in, lor_out, small_sems.at[1]),
    ]
    for copy in smalls:
        copy.start()

    def store(at):
        return pltpu.make_async_copy(
            held.at[:, pl.ds(at, 1)], out.at[:, pl.ds(at, 1)], sems.at[at]
        )

    def layer(at, carry):
        word = words[at]
        held[0, at] = post[slot_of[0], at + 1, own]
        for i in range(1, 19):
            step_x, step_y, step_z = lattice_dirs[i]
            pulled = post[slot_of[i], at + 1 - step_z, pl.ds(SIDE - step_y, size_y)]
            if step_x != 0:
                pulled = pltpu.roll(pulled, step_x % size_x, 1)
            taken = (word & bit_of(step_x, step_y, step_z)) != 0
            held[i, at] = jnp.where(taken, pulled, post[slot_of[opposite_dir[i]], at + 1, own])
        store(at).start()
        return carry

    lax.fori_loop(0, size_z, layer, 0)

    def finish(at, carry):
        store(at).wait()
        return carry

    lax.fori_loop(0, size_z, finish, 0)
    for copy in smalls:
        copy.wait()


def per_device(populations, flags, potential, conductivity, coil_phase, phase_table, magnetic):
    size_z, size_y, size_x = flags.shape
    rough_z, rough_y, rough_x = potential.shape
    assert rough_x * 2 <= 128 and rough_z >= REACH and 11 <= rough_y <= 13
    vmem = pl.BlockSpec(memory_space=pltpu.VMEM)
    hbm = pl.BlockSpec(memory_space=pltpu.HBM)
    ext = (size_z + 2, size_y + 2 * SIDE, size_x)
    f32, i32 = jnp.float32, jnp.int32
    post, words, potential_now, lorentz = pl.pallas_call(
        exchange_kernel,
        out_shape=(
            pltpu.VMEM((19,) + ext, f32),
            pltpu.VMEM(flags.shape, i32),
            pltpu.VMEM(potential.shape, f32),
            pltpu.VMEM(magnetic.shape, f32),
        ),
        in_specs=[hbm] * 7,
        out_specs=(vmem,) * 4,
        scratch_shapes=[
            pltpu.VMEM(populations.shape, f32),
            pltpu.VMEM(potential.shape, f32),
            pltpu.VMEM(potential.shape, f32),
            pltpu.VMEM(potential.shape, i32),
            pltpu.VMEM(magnetic.shape, f32),
            pltpu.VMEM(phase_table.shape, f32),
            pltpu.VMEM((rough_z, 16, 128), f32),
            pltpu.VMEM((8, rough_z, 16, 128), f32),
            pltpu.VMEM(ext, i32),
            pltpu.VMEM(ext[1:], i32),
            pltpu.VMEM((size_z + 2, size_y, size_x), i32),
            pltpu.VMEM((2, 5, -(-size_z // 8) * 8, size_x), f32),
            pltpu.VMEM((2, 5, -(-size_z // 8) * 8, size_x), f32),
            pltpu.VMEM((3 * rough_z, 16, 128), f32),
            pltpu.VMEM((3, rough_z, size_y, size_x), f32),
            pltpu.SemaphoreType.DMA((9,)),
        ]
        + [pltpu.SemaphoreType.DMA((8,))] * 6,
        compiler_params=pltpu.CompilerParams(
            collective_id=0, has_side_effects=True, vmem_limit_bytes=24 * 2**20
        ),
        name="exchange_and_collide",
    )(
        *(
            pltpu.with_memory_space_constraint(x, pltpu.HBM)
            for x in (
                populations, flags, potential, conductivity, coil_phase, magnetic, phase_table
            )
        )
    )
    result, potential_now, lorentz = pl.pallas_call(
        stream_kernel,
        out_shape=(
            jax.ShapeDtypeStruct(populations.shape, f32),
            jax.ShapeDtypeStruct(potential.shape, f32),
            jax.ShapeDtypeStruct(magnetic.shape, f32),
        ),
        in_specs=[vmem] * 4,
        out_specs=(hbm,) * 3,
        scratch_shapes=[
            pltpu.VMEM(populations.shape, f32),
            pltpu.SemaphoreType.DMA((size_z,)),
            pltpu.SemaphoreType.DMA((2,)),
        ],
        compiler_params=pltpu.CompilerParams(vmem_limit_bytes=24 * 2**20),
        name="stream",
    )(
        *(
            pltpu.with_memory_space_constraint(x, pltpu.VMEM)
            for x in (post, words, potential_now, lorentz)
        )
    )
    return (result, potential_now, lorentz)


def solution(mesh):
    in_specs = (
        P(None, ("groups", "wide"), "narrow", None),
        P(("groups", "wide"), "narrow", None),
        P(("groups", "wide"), "narrow", None),
        P(("groups", "wide"), "narrow", None),
        P(("groups", "wide"), "narrow", None),
        P(),
        P(None, ("groups", "wide"), "narrow", None),
    )
    out_specs = (
        P(None, ("groups", "wide"), "narrow", None),
        P(("groups", "wide"), "narrow", None),
        P(None, ("groups", "wide"), "narrow", None),
    )
    return jax.shard_map(
        per_device, mesh=mesh, in_specs=in_specs, out_specs=out_specs, check_vma=False
    )
```

profile of v0, /device:TPU:0, one launch (start us, length us, event | category | flops | bytes accessed | tf_op | source)
XLA Modules:
  0.0 17.5 jit_solution(1930758739440760251)
XLA Ops:
  0.6 14.2 %exchange_and_collide.1 = (f32[19,14,64,128]{3,2,1,0:T(8,128)S(1)}, s32[12,48,128]{2,1,0:T(8,128)S(1)}, f32[3,12,32]{2,1,0:T(8,128)S(1)}, f32[3,3,12,32]{3,2,1,0:T(8,128)S(1)}) custom-call(f32[19,12,48,128]{3,2,1,0:T(8,128)} %pop_hbm.1, s32[12,48,128]{2,1,0:T(8,128)} %flags_hbm.1, f32[3,12,32]{2,1,0:T(8,128)} %pot_hbm.1, f32[3,12,32]{2,1,0:T(8,128)} %cond_hbm.1, ...), custom_call_target="tpu_custom_call" | custom-call | tf_op jit(solution)/shard_map/exchange_and_collide/pallas_call | solution.py:494
  14.8 2.7 %stream.1 = (f32[19,12,48,128]{3,2,1,0:T(8,128)}, f32[3,12,32]{2,1,0:T(8,128)}, f32[3,3,12,32]{3,2,1,0:T(8,128)}) custom-call(f32[19,14,64,128]{3,2,1,0:T(8,128)S(1)} %get-tuple-element.7.post, s32[12,48,128]{2,1,0:T(8,128)S(1)} %get-tuple-element.8.words, f32[3,12,32]{2,1,0:T(8,128)S(1)} %get-tuple-element.9.pot_in, ...), custom_call_target="tpu_custom_call" | custom-call | tf_op jit(solution)/shard_map/stream/pallas_call | solution.py:535
where the time goes:
time: 17.7 us; the launch traced here: 17.5 us
  Pallas kernels  16.9 us (95%)
  between operations  0.64 us (4%)
    pallas_call x1, Pallas kernels, per_device(): pl.pallas_call(exchange_kernel, out_shape=(pltpu.VMEM((19,) + ext, f32),...  14.2 us
    pallas_call x1, Pallas kernels, per_device(): pl.pallas_call(stream_kernel, out_shape=(jax.ShapeDtypeStruct(populations...  2.69 us

commit v1 on v0

--- a/solution.py
+++ b/solution.py
@@ -104,7 +104,7 @@
         copy.start()
         smalls.append(copy)
     loads = []
-    spans = [(0, 1), (size_z - 1, 1), (1, size_z - 2)]
+    spans = [(size_z - 1, 1), (0, 1), (1, size_z - 2)]
     for number, (first, count) in enumerate(spans):
         copy = pltpu.make_async_copy(
             pop_hbm.at[:, pl.ds(first, count)], popv.at[:, pl.ds(first, count)], in_sems.at[number]
@@ -297,7 +297,7 @@
         spread,
         precision=lax.Precision.HIGHEST,
         preferred_element_type=jnp.float32,
-    ) * force_scale
+    ) * (0.5 * force_scale)
     wide_sub = lax.broadcasted_iota(jnp.int32, (8, size_x), 0)
     for place in range(3 * rough_z):
         for tile in range(tiles):
@@ -316,50 +316,58 @@
         out_rows = pl.ds(first + SIDE, 8)
         f = [popv[i, at, rows] for i in range(19)]
         kind = cells[at + 1, out_rows]
-        forces = [force[a, lax.div(at, up_z), rows] for a in range(3)]
+        half_force = [force[a, at // up_z if isinstance(at, int) else lax.div(at, up_z), rows] for a in range(3)]
         fluid = kind == 0
         wall = kind == 1
         inlet = kind == 2
+        pairs = range(1, 19, 2)
+        both = {i: f[i] + f[i + 1] for i in pairs}
+        apart = {i: f[i] - f[i + 1] for i in pairs}
         density = f[0]
         mom = [None, None, None]
-        for i in range(1, 19, 2):
-            both = f[i] + f[i + 1]
-            apart = f[i] - f[i + 1]
-            density = density + both
+        for i in pairs:
+            density = density + both[i]
             for a in range(3):
                 step = lattice_dirs[i][a]
                 if step != 0:
-                    part = apart if step > 0 else -apart
-                    mom[a] = part if mom[a] is None else (
-                        mom[a] + apart if step > 0 else mom[a] - apart
+                    mom[a] = apart[i] if mom[a] is None else (
+                        mom[a] + apart[i] if step > 0 else mom[a] - apart[i]
                     )
         inverse = 1.0 / density
         still = (0.0, 0.0, -inlet_speed)
         vel = [
-            jnp.where(inlet, jnp.float32(still[a]), (mom[a] + 0.5 * forces[a]) * inverse)
+            jnp.where(inlet, jnp.float32(still[a]), (mom[a] + half_force[a]) * inverse)
             for a in range(3)
         ]
-        scale = jnp.where(fluid, density * (1.0 / relax_time), jnp.where(wall, 0.0, 1.0))
-        kept = jnp.where(fluid, jnp.float32(keep), jnp.where(wall, 1.0, 0.0))
-        push = [jnp.where(fluid, (3.0 * share) * forces[a], 0.0) for a in range(3)]
-        square = vel[0] * vel[0] + vel[1] * vel[1] + vel[2] * vel[2]
+        small = lattice_weights[-1]
+        scale = jnp.where(fluid, density * (small / relax_time), jnp.where(wall, 0.0, small))
+        kept_even = jnp.where(fluid, jnp.float32(0.5 * keep), jnp.where(wall, 0.5, 0.0))
+        kept_odd = jnp.where(wall, jnp.float32(-0.5), kept_even)
+        push = [jnp.where(fluid, (6.0 * share * small) * half_force[a], 0.0) for a in range(3)]
+        vel15 = [1.5 * vel[a] for a in range(3)]
+        square = vel15[0] * vel[0] + vel15[1] * vel[1] + vel15[2] * vel[2]
         work = vel[0] * push[0] + vel[1] * push[1] + vel[2] * push[2]
-        base = scale - (1.5 * scale) * square - work
+        base = scale - scale * square - work
         scale3 = 3.0 * scale
+        line = [scale3 * vel[a] + push[a] for a in range(3)]
+        line_more = [line[a] + push[a] for a in range(3)]
         result = [None] * 19
-        result[0] = kept * f[0] + lattice_weights[0] * base
-        based = {w: w * base for w in set(lattice_weights[1:])}
-        for i in range(1, 19, 2):
-            w = lattice_weights[i]
-            along_u = signed_sum(lattice_dirs[i], vel)
-            along_f = signed_sum(lattice_dirs[i], push)
-            odd = scale3 * along_u + along_f
-            even = based[w] + (1.5 * w) * along_u * (odd + along_f)
-            odd = w * odd
-            one, two = kept * f[i], kept * f[i + 1]
-            one, two = jnp.where(wall, two, one), jnp.where(wall, one, two)
-            result[i] = one + (even + odd)
-            result[i + 1] = two + (even - odd)
+        result[0] = (2.0 * kept_even) * f[0] + 12.0 * base
+        base2 = 2.0 * base
+        for i in pairs:
+            steps = lattice_dirs[i]
+            along = signed_sum(steps, vel15)
+            odd = signed_sum(steps, line)
+            more = along * signed_sum(steps, line_more)
+            if i < 7:
+                odd = 2.0 * odd
+                even = base2 + 2.0 * more
+            else:
+                even = base + more
+            even = kept_even * both[i] + even
+            odd = kept_odd * apart[i] + odd
+            result[i] = even + odd
+            result[i + 1] = even - odd
         for i in range(19):
             post[slot_of[i], at + 1, out_rows] = result[i]
         if edge != 0:
@@ -368,21 +376,15 @@
                 ysend[side, k, pl.ds(at, 1)] = result[i][pick : pick + 1]
 
     last = size_y - 8
-    loads[0].wait()
-    loads[1].wait()
-
-    def ends(turn, carry):
-        at = turn * (size_z - 1)
+    for load, at, out_z in ((0, size_z - 1, 1), (1, 0, -1)):
+        loads[load].wait()
         block(at, 0, -1)
         for tile in range(1, tiles - 1):
             block(at, tile * 8, 0)
         block(at, last, 1)
-        return carry
-
-    lax.fori_loop(0, 2, ends, 0)
-    for number, way in enumerate(ways):
-        if way[0] != 0:
-            start(post_copy, number)
+        for number, way in enumerate(ways):
+            if way[0] == out_z:
+                start(post_copy, number)
     loads[2].wait()
 
     def sides(at, carry):
@@ -450,25 +452,27 @@
     smalls = [
         pltpu.make_async_copy(pot_in, pot_out, small_sems.at[0]),
         pltpu.make_async_copy(lor_in, lor_out, small_sems.at[1]),
+        pltpu.make_async_copy(
+            post.at[slot_of[0], pl.ds(1, size_z), own], out.at[0], small_sems.at[2]
+        ),
     ]
     for copy in smalls:
         copy.start()
 
     def store(at):
         return pltpu.make_async_copy(
-            held.at[:, pl.ds(at, 1)], out.at[:, pl.ds(at, 1)], sems.at[at]
+            held.at[:, pl.ds(at, 1)], out.at[pl.ds(1, 18), pl.ds(at, 1)], sems.at[at]
         )
 
     def layer(at, carry):
         word = words[at]
-        held[0, at] = post[slot_of[0], at + 1, own]
         for i in range(1, 19):
             step_x, step_y, step_z = lattice_dirs[i]
             pulled = post[slot_of[i], at + 1 - step_z, pl.ds(SIDE - step_y, size_y)]
             if step_x != 0:
                 pulled = pltpu.roll(pulled, step_x % size_x, 1)
             taken = (word & bit_of(step_x, step_y, step_z)) != 0
-            held[i, at] = jnp.where(taken, pulled, post[slot_of[opposite_dir[i]], at + 1, own])
+            held[i - 1, at] = jnp.where(taken, pulled, post[slot_of[opposite_dir[i]], at + 1, own])
         store(at).start()
         return carry
 
@@ -542,9 +546,9 @@
         in_specs=[vmem] * 4,
         out_specs=(hbm,) * 3,
         scratch_shapes=[
-            pltpu.VMEM(populations.shape, f32),
+            pltpu.VMEM((18,) + flags.shape, f32),
             pltpu.SemaphoreType.DMA((size_z,)),
-            pltpu.SemaphoreType.DMA((2,)),
+            pltpu.SemaphoreType.DMA((3,)),
         ],
         compiler_params=pltpu.CompilerParams(vmem_limit_bytes=24 * 2**20),
         name="stream",

time: 17.7 us -> 17.5 us (0.989)
  Pallas kernels: 16.9 us -> 16.7 us
where the time goes in v1:
time: 17.5 us; the launch traced here: 17.4 us
  Pallas kernels  16.7 us (95%)
  between operations  0.64 us (4%)
    pallas_call x1, Pallas kernels, per_device(): pl.pallas_call(exchange_kernel, out_shape=(pltpu.VMEM((19,) + ext, f32),...  14.1 us
    pallas_call x1, Pallas kernels, per_device(): pl.pallas_call(stream_kernel, out_shape=(jax.ShapeDtypeStruct(populations...  2.61 us

profile of v1, /device:TPU:0, one launch (start us, length us, event | category | flops | bytes accessed | tf_op | source)
XLA Modules:
  0.0 17.4 jit_solution(14777008697596202448)
XLA Ops:
  0.6 14.1 %exchange_and_collide.1 = (f32[19,14,64,128]{3,2,1,0:T(8,128)S(1)}, s32[12,48,128]{2,1,0:T(8,128)S(1)}, f32[3,12,32]{2,1,0:T(8,128)S(1)}, f32[3,3,12,32]{3,2,1,0:T(8,128)S(1)}) custom-call(f32[19,12,48,128]{3,2,1,0:T(8,128)} %pop_hbm.1, s32[12,48,128]{2,1,0:T(8,128)} %flags_hbm.1, f32[3,12,32]{2,1,0:T(8,128)} %pot_hbm.1, f32[3,12,32]{2,1,0:T(8,128)} %cond_hbm.1, ...), custom_call_target="tpu_custom_call" | custom-call | tf_op jit(solution)/shard_map/exchange_and_collide/pallas_call | solution.py:498
  14.8 2.6 %stream.1 = (f32[19,12,48,128]{3,2,1,0:T(8,128)}, f32[3,12,32]{2,1,0:T(8,128)}, f32[3,3,12,32]{3,2,1,0:T(8,128)}) custom-call(f32[19,14,64,128]{3,2,1,0:T(8,128)S(1)} %get-tuple-element.7.post, s32[12,48,128]{2,1,0:T(8,128)S(1)} %get-tuple-element.8.words, f32[3,12,32]{2,1,0:T(8,128)S(1)} %get-tuple-element.9.pot_in, ...), custom_call_target="tpu_custom_call" | custom-call | tf_op jit(solution)/shard_map/stream/pallas_call | solution.py:539

commit v2 on v1

--- a/solution.py
+++ b/solution.py
@@ -288,24 +288,21 @@
             lor_out[a, layer] = value
             lor_rows[a * rough_z + layer, 0:rough_y, 0:rough_x] = value
 
-    spread_from = lax.broadcasted_iota(jnp.int32, (128, size_x), 0)
-    spread_to = lax.broadcasted_iota(jnp.int32, (128, size_x), 1)
-    first_lane = spread_from * up_x
-    spread = ((spread_to >= first_lane) & (spread_to < first_lane + up_x)).astype(jnp.float32)
-    wide_rows = jnp.dot(
-        lor_rows[...].reshape(3 * rough_z * 16, 128),
-        spread,
-        precision=lax.Precision.HIGHEST,
-        preferred_element_type=jnp.float32,
-    ) * (0.5 * force_scale)
+    wide_lane = lax.broadcasted_iota(jnp.int32, (8, size_x), 1)
     wide_sub = lax.broadcasted_iota(jnp.int32, (8, size_x), 0)
+    from_lane = lax.div(wide_lane, jnp.full((8, size_x), up_x, jnp.int32))
     for place in range(3 * rough_z):
+        spread = [
+            jnp.take_along_axis(lor_rows[place, first : first + 8], from_lane, axis=1)
+            * (0.5 * force_scale)
+            for first in (0, 8)
+        ]
         for tile in range(tiles):
             value = None
             for part in range(8 // up_y):
-                at = place * 16 + tile * (8 // up_y) + part
-                line = jnp.broadcast_to(wide_rows[at : at + 1], (8, size_x))
-                value = line if value is None else jnp.where(wide_sub < part * up_y, value, line)
+                at = tile * (8 // up_y) + part
+                one = jnp.broadcast_to(spread[at // 8][at % 8 : at % 8 + 1], (8, size_x))
+                value = one if value is None else jnp.where(wide_sub < part * up_y, value, one)
             force[place // rough_z, place % rough_z, tile * 8 : tile * 8 + 8] = value
 
     share = 1.0 - 0.5 / relax_time

time: 17.5 us -> 17.4 us (level)
  no operation moved by 1% of the time
where the time goes in v2:
time: 17.4 us; the launch traced here: 17.3 us
  Pallas kernels  16.6 us (95%)
  between operations  0.64 us (4%)
    pallas_call x1, Pallas kernels, per_device(): pl.pallas_call(exchange_kernel, out_shape=(pltpu.VMEM((19,) + ext, f32),...  14 us
    pallas_call x1, Pallas kernels, per_device(): pl.pallas_call(stream_kernel, out_shape=(jax.ShapeDtypeStruct(populations...  2.61 us

profile of v2, /device:TPU:0, one launch (start us, length us, event | category | flops | bytes accessed | tf_op | source)
XLA Modules:
  0.0 17.3 jit_solution(8306806818975064599)
XLA Ops:
  0.6 14.0 %exchange_and_collide.1 = (f32[19,14,64,128]{3,2,1,0:T(8,128)S(1)}, s32[12,48,128]{2,1,0:T(8,128)S(1)}, f32[3,12,32]{2,1,0:T(8,128)S(1)}, f32[3,3,12,32]{3,2,1,0:T(8,128)S(1)}) custom-call(f32[19,12,48,128]{3,2,1,0:T(8,128)} %pop_hbm.1, s32[12,48,128]{2,1,0:T(8,128)} %flags_hbm.1, f32[3,12,32]{2,1,0:T(8,128)} %pot_hbm.1, f32[3,12,32]{2,1,0:T(8,128)} %cond_hbm.1, ...), custom_call_target="tpu_custom_call" | custom-call | tf_op jit(solution)/shard_map/exchange_and_collide/pallas_call | solution.py:495
  14.7 2.6 %stream.1 = (f32[19,12,48,128]{3,2,1,0:T(8,128)}, f32[3,12,32]{2,1,0:T(8,128)}, f32[3,3,12,32]{3,2,1,0:T(8,128)}) custom-call(f32[19,14,64,128]{3,2,1,0:T(8,128)S(1)} %get-tuple-element.7.post, s32[12,48,128]{2,1,0:T(8,128)S(1)} %get-tuple-element.8.words, f32[3,12,32]{2,1,0:T(8,128)S(1)} %get-tuple-element.9.pot_in, ...), custom_call_target="tpu_custom_call" | custom-call | tf_op jit(solution)/shard_map/stream/pallas_call | solution.py:536

commit v3 on v2

--- a/solution.py
+++ b/solution.py
@@ -224,13 +224,13 @@
 
     for number in range(8):
         start(rough_copy, number)
+
     smalls[4].wait()
+    smalls[5].wait()
+    for number in range(8):
+        wait_received(rough_copy, number)
     for number in range(8):
         start(flag_copy, number)
-    smalls[5].wait()
-
-    for number in range(8):
-        wait_received(rough_copy, number)
 
     tall = 3 * 8
     row = lax.broadcasted_iota(jnp.int32, (tall, 128), 0)
@@ -424,7 +424,7 @@
 
     lax.fori_loop(0, size_z, join, 0)
 
-    for number in range(8):
+    for number in (2, 3):
         wait_received(post_copy, number)
     for way, row_at in ((1, SIDE - 1), (-1, SIDE + size_y)):
         side = 0 if way > 0 else 1
@@ -435,6 +435,9 @@
     for number in range(8):
         wait_sent(rough_copy, number)
         wait_sent(flag_copy, number)
+    for number in (0, 1, 4, 5, 6, 7):
+        wait_received(post_copy, number)
+    for number in range(8):
         wait_sent(post_copy, number)
 
 

time: 17.4 us -> 17.2 us (0.989)
  Pallas kernels: 16.6 us -> 16.4 us
    pallas_call x1, Pallas kernels: 14 us -> 13.8 us  [per_device(): pl.pallas_call(exchange_kernel, out_shape=(pltpu.VMEM((19,) + ext, f32),...]
where the time goes in v3:
time: 17.2 us; the launch traced here: 17.1 us
  Pallas kernels  16.4 us (95%)
  between operations  0.64 us (4%)
    pallas_call x1, Pallas kernels, per_device(): pl.pallas_call(exchange_kernel, out_shape=(pltpu.VMEM((19,) + ext, f32),...  13.8 us
    pallas_call x1, Pallas kernels, per_device(): pl.pallas_call(stream_kernel, out_shape=(jax.ShapeDtypeStruct(populations...  2.61 us

profile of v3, /device:TPU:0, one launch (start us, length us, event | category | flops | bytes accessed | tf_op | source)
XLA Modules:
  0.0 17.1 jit_solution(9277435517074259901)
XLA Ops:
  0.6 13.8 %exchange_and_collide.1 = (f32[19,14,64,128]{3,2,1,0:T(8,128)S(1)}, s32[12,48,128]{2,1,0:T(8,128)S(1)}, f32[3,12,32]{2,1,0:T(8,128)S(1)}, f32[3,3,12,32]{3,2,1,0:T(8,128)S(1)}) custom-call(f32[19,12,48,128]{3,2,1,0:T(8,128)} %pop_hbm.1, s32[12,48,128]{2,1,0:T(8,128)} %flags_hbm.1, f32[3,12,32]{2,1,0:T(8,128)} %pot_hbm.1, f32[3,12,32]{2,1,0:T(8,128)} %cond_hbm.1, ...), custom_call_target="tpu_custom_call" | custom-call | tf_op jit(solution)/shard_map/exchange_and_collide/pallas_call | solution.py:498
  14.5 2.6 %stream.1 = (f32[19,12,48,128]{3,2,1,0:T(8,128)}, f32[3,12,32]{2,1,0:T(8,128)}, f32[3,3,12,32]{3,2,1,0:T(8,128)}) custom-call(f32[19,14,64,128]{3,2,1,0:T(8,128)S(1)} %get-tuple-element.7.post, s32[12,48,128]{2,1,0:T(8,128)S(1)} %get-tuple-element.8.words, f32[3,12,32]{2,1,0:T(8,128)S(1)} %get-tuple-element.9.pot_in, ...), custom_call_target="tpu_custom_call" | custom-call | tf_op jit(solution)/shard_map/stream/pallas_call | solution.py:539
